TPU v7x, 256 devices: a whole 4x4x8 slice. The times are simulated.
256 devices in a mesh: seq: 8 (over y, z_lo), head: 32 (over x, z_hi, core).
Axes of the slice: x: 4, y: 4, z: 8 (z_hi: 4, z_lo: 2; z = z_hi * 2 + z_lo), core: 2. Of those that a mesh axis runs over, the one named last changes fastest.
Arguments:
- queries: bfloat16 [2048, 128, 576], P('seq', 'head'), may hold values from -200 to 200
- latent_cache: bfloat16 [2048, 576], P('seq'), may hold values from -6 to 6
- grad_output: bfloat16 [2048, 128, 512], P('seq', 'head'), may hold values from -6 to 6
- query_blocks: int32 [8], replicated, may hold values from 0 to 127, as said below
- key_blocks: int32 [8], replicated, may hold values from 0 to 127, as said below
Outputs:
- grad_queries: bfloat16 [2048, 128, 576], P('seq', 'head')
- grad_cache: float32 [2048, 576], P(('seq', 'head'))
Inputs may be any that keep to these rules, and one draw needn't show every extreme that they name: `query_blocks`: the groups hold distinct block positions, one of them 16 * 8 - 1. `key_blocks`: the groups hold distinct block positions, one of them 0 and one 16 * 8 - 1.
All inputs are finite; a program needn't handle non-finite values.
Results may differ from a plain program's by a relative error of at most 0.013.
Values may be sent and summed in bfloat16 or wider, within the bound.
No kernel may reach another device: no remote copies, remote signals or barrier semaphores. Data moves between devices by JAX's collectives and lax.ppermute only.
A program may use at most 64 MiB of HBM per device.

v0:
```python
import jax
import jax.numpy as jnp
from jax import lax
from jax.sharding import PartitionSpec as P

DL = 512
DR = 64
softmax_scale = 0.07216878364870322


def shards(queries, latent_cache, grad_output, query_blocks, key_blocks):
    gathered = lax.all_gather(latent_cache, "seq", axis=0, tiled=True)
    tile_rows = queries.shape[0]
    group_index = lax.axis_index("seq")
    offsets = jnp.arange(tile_rows, dtype=jnp.int32)
    query_pos = query_blocks[group_index] * tile_rows + offsets
    key_pos = (key_blocks[:, None] * tile_rows + offsets[None, :]).reshape(-1)
    values = gathered[:, :DL]
    scores = softmax_scale * jnp.einsum(
        "qhd,kd->qhk", queries, gathered, preferred_element_type=jnp.float32
    )
    visible = key_pos[None, None, :] <= query_pos[:, None, None]
    masked = jnp.where(visible, scores, -jnp.inf)
    row_max = jnp.max(masked, axis=-1, keepdims=True)
    weights = jnp.exp(masked - row_max)
    probability = weights / jnp.sum(weights, axis=-1, keepdims=True)
    prob_bf16 = probability.astype(jnp.bfloat16)
    grad_probs = jnp.einsum("qhe,ke->qhk", grad_output, values, preferred_element_type=jnp.float32)
    output = jnp.einsum("qhk,ke->qhe", prob_bf16, values, preferred_element_type=jnp.float32)
    correction = jnp.sum(grad_output.astype(jnp.float32) * output, axis=-1, keepdims=True)
    grad_scores = (softmax_scale * probability * (grad_probs - correction)).astype(jnp.bfloat16)
    grad_queries = jnp.einsum(
        "qhk,kd->qhd", grad_scores, gathered, preferred_element_type=jnp.float32
    ).astype(jnp.bfloat16)
    grad_keys = jnp.einsum("qhk,qhd->kd", grad_scores, queries, preferred_element_type=jnp.float32)
    grad_values = jnp.einsum(
        "qhk,qhe->ke", prob_bf16, grad_output, preferred_element_type=jnp.float32
    )
    zeros_rope = jnp.zeros((grad_values.shape[0], DR), jnp.float32)
    partial_value = grad_keys + jnp.concatenate([grad_values, zeros_rope], axis=1)
    grad_cache = lax.psum_scatter(partial_value, ("seq", "head"), scatter_dimension=0, tiled=True)
    return (grad_queries, grad_cache)


def solution(mesh):
    placed = (P("seq", "head", None), P("seq", None), P("seq", "head", None), P(), P())
    return jax.shard_map(
        shards,
        mesh=mesh,
        in_specs=placed,
        out_specs=(P("seq", "head", None), P(("seq", "head"), None)),
        check_vma=False,
    )
```

profile of v0, /device:TPU:2, one launch (start us, length us, event | category | flops | bytes accessed | tf_op | source)
XLA Modules:
  0.0 385.2 jit_solution(10992031810698439277)
XLA Ops:
  7.2 0.0 copy-start
  7.2 0.0 all-gather.2.cloned.1.call-start
  7.2 0.7 all-gather.2.cloned.1.call-update
  7.9 0.0 all-reduce.4.cloned.1.call-start
  8.0 0.7 broadcast_multiply_fusion
  8.6 0.1 add_bitcast_fusion
  8.7 1.2 dynamic_slice.3
  10.6 0.4 broadcast_compare_fusion
  11.0 59.7 %all-gather.2.cloned.1.call-done = bf16[2048,576]{0,1:T(8,128)(2,1)} async-done(((bf16[256,576]{0,1:T(8,128)(2,1)}), bf16[2048,576]{0,1:T(8,128)(2,1)}) %all-gather.2.cloned.1.call-update) | async-done | bytes 2359312 | tf_op jit(solution)/shard_map/all_gather | solution.py:12
  70.7 0.0 copy-done
  70.7 7.3 %fusion.8 = f32[256,4,2048]{2,0,1:T(8,128)} fusion(bf16[256,4,576]{0,2,1:T(8,128)(2,1)S(1)} %copy-done, bf16[2048,576]{0,1:T(8,128)(2,1)} %all-gather.2.cloned.1.call-done), kind=kOutput, calls=%fused_computation.14 | convolution fusion | flops 2415919104 | bytes 11927552 | tf_op jit(solution)/shard_map/qhd,kd->qhk/dot_general | solution.py:19
  78.0 9.4 %fusion.17 = (f32[256,4]{0,1:T(4,128)S(1)}, f32[256,4,2048]{2,0,1:T(8,128)S(1)}) fusion(f32[256,4,2048]{2,0,1:T(8,128)} %fusion.8, pred[256,2048]{1,0:T(8,128)(4,1)S(1)} %broadcast_compare_fusion), kind=kOutput, calls=%fused_computation.28 | output fusion | flops 12584959 | bytes 17305600 | tf_op jit(solution)/shard_map/sub | solution.py:25
  87.4 0.0 copy-start.2
  87.4 1.4 fusion.5
  88.8 0.0 copy-done.2
  88.8 0.0 copy-start.1
  88.8 2.5 convolution_bitcast_fusion
  91.3 0.0 copy-done.1
  91.3 2.5 multiply_reduce_fusion
  93.8 3.3 multiply_convert_fusion
  97.1 0.0 copy-start.3
  97.1 2.1 copy-done.3
  99.2 5.3 %bitcast_add_fusion = f32[2048,576]{1,0:T(8,128)} fusion(f32[2048,512]{1,0:T(8,128)S(1)} %convolution_bitcast_fusion, bf16[256,4,2048]{2,0,1:T(8,128)(2,1)S(1)} %multiply_convert_fusion, bf16[256,4,576]{0,2,1:T(8,128)(2,1)S(1)} %copy-done), kind=kOutput, calls=%fused_computation.5 | convolution fusion | flops 2417098752 | bytes 14286848 | tf_op jit(solution)/shard_map/qhk,qhd->kd/dot_general | solution.py:35
  104.5 0.0 all-reduce.4.cloned.1.call-update
  104.5 5.8 %fusion.10 = bf16[256,4,576]{0,2,1:T(8,128)(2,1)} fusion(bf16[256,4,2048]{2,0,1:T(8,128)(2,1)} %copy-done.3, bf16[2048,576]{0,1:T(8,128)(2,1)S(1)} %copy-done.1), kind=kOutput, calls=%fused_computation.18 | convolution fusion | flops 2416508928 | bytes 7733248 | tf_op jit(solution)/shard_map/qhk,kd->qhd/dot_general | solution.py:32
  110.4 266.7 %all-reduce.4.cloned.1.call-done = f32[2048,576]{1,0:T(8,128)} async-done(((f32[2048,576]{1,0:T(8,128)}), f32[2048,576]{1,0:T(8,128)}) %all-reduce.4.cloned.1.call-update) | async-done | bytes 4718608
  377.0 1.3 constant_dynamic-slice_fusion
  (2 shorter events, 0.0 us)
Async XLA Ops:
  7.2 63.5 %copy-start = (bf16[256,4,576]{0,2,1:T(8,128)(2,1)S(1)}, bf16[256,4,576]{0,2,1:T(8,128)(2,1)}, u32[]{:S(2)}) copy-start(bf16[256,4,576]{0,2,1:T(8,128)(2,1)} %param.5) | copy-start | bytes 3538948
  7.2 63.5 %all-gather.2.cloned.1.call-start = ((), (), s32[]{:S(2)}) async-start(), calls=%async_computation | async-start | bytes 2654208 | tf_op jit(solution)/shard_map/all_gather | solution.py:12
  7.9 369.1 %all-reduce.4.cloned.1.call-start = ((), (), s32[]{:S(2)}) async-start(), calls=%async_computation.1 | async-start | bytes 10485760
  87.4 1.4 copy-start.2
  88.8 2.5 copy-start.1
  97.1 2.1 copy-start.3
Sparse Core Ops, SparseCore 0:
  9.7 60.8 all-gather.1
  104.6 272.3 all-reduce.3
where the time goes:
time: 385 us
  waiting for transfers between devices  327 us (85%)
  matrix products  26.7 us (7%)
  between operations  14.8 us (4%)
  other arithmetic  11.9 us (3%)
  local copies, waits for them, and re-layouts  4.67 us (1%)
    unnamed x3, waiting for transfers between devices  267 us
    all_gather x1, waiting for transfers between devices, shards(): gathered = lax.all_gather(latent_cache, 'seq', axis=0, tiled=True)  59.7 us
    sub x1, other arithmetic, shards(): weights = jnp.exp(masked - row_max)  9.45 us
  transfers between devices with their start and end apart: 2, of which 2 were waited for; matrix products, arithmetic and copies ran while one was open for 2% of the time, Pallas kernels for 0%

commit v1 on v0

--- a/solution.py
+++ b/solution.py
@@ -9,7 +9,9 @@
 
 
 def shards(queries, latent_cache, grad_output, query_blocks, key_blocks):
-    gathered = lax.all_gather(latent_cache, "seq", axis=0, tiled=True)
+    gathered = jnp.concatenate(
+        lax.all_to_all(jnp.stack([latent_cache] * lax.axis_size("seq")), "seq", 0, 0), axis=0
+    )
     tile_rows = queries.shape[0]
     group_index = lax.axis_index("seq")
     offsets = jnp.arange(tile_rows, dtype=jnp.int32)

time: 385 us -> 367 us (0.953)
  waiting for transfers between devices: 327 us -> 292 us
  local copies, waits for them, and re-layouts: 4.67 us -> 17.8 us
  other arithmetic: 11.9 us -> 5.94 us
  starting transfers between devices: 0.08 us -> 5.86 us
    all_gather x1 -> x0, waiting for transfers between devices: 59.7 us -> none  [shards(): gathered = lax.all_gather(latent_cache, 'seq', axis=0, tiled=True)]
    all_to_all x0 -> x1, waiting for transfers between devices: none -> 27.2 us  [shards(): lax.all_to_all(jnp.stack([latent_cache] * lax.axis_size('seq')), 'seq', 0...]
    sub x0 -> x1, matrix products: none -> 10.2 us  [shards(): weights = jnp.exp(masked - row_max)]
    sub x1 -> x0, other arithmetic: 9.45 us -> none  [shards(): weights = jnp.exp(masked - row_max)]
    dot_general x1 -> x0, matrix products: 7.3 us -> none  [shards(): jnp.einsum('qhd,kd->qhk', queries, gathered, preferred_element_type=jnp.f...]
    reshape x0 -> x2, local copies, waits for them, and re-layouts: none -> 6.77 us  [shards(): jnp.concatenate(lax.all_to_all(jnp.stack([latent_cache] * lax.axis_size('...]
    all_to_all x0 -> x1, starting transfers between devices: none -> 5.82 us  [shards(): lax.all_to_all(jnp.stack([latent_cache] * lax.axis_size('seq')), 'seq', 0...]
    unnamed x3 -> x2, waiting for transfers between devices: 267 us -> 265 us
where the time goes in v1:
time: 367 us; the launch traced here: 366 us
  waiting for transfers between devices  292 us (80%)
  matrix products  29.6 us (8%)
  local copies, waits for them, and re-layouts  17.8 us (5%)
  between operations  14.8 us (4%)
  other arithmetic  5.94 us (2%)
  starting transfers between devices  5.86 us (2%)
    unnamed x2, waiting for transfers between devices  265 us
    all_to_all x1, waiting for transfers between devices, shards(): lax.all_to_all(jnp.stack([latent_cache] * lax.axis_size('seq')), 'seq', 0...  27.2 us
    sub x1, matrix products, shards(): weights = jnp.exp(masked - row_max)  10.2 us
  transfers between devices with their start and end apart: 2, of which 2 were waited for; matrix products, arithmetic and copies ran while one was open for 2% of the time, Pallas kernels for 0%

profile of v1, /device:TPU:2, one launch (start us, length us, event | category | flops | bytes accessed | tf_op | source)
XLA Modules:
  0.0 366.1 jit_solution(1121639650477886250)
XLA Ops:
  7.2 0.0 copy-start
  7.2 0.0 copy-start.4
  7.2 0.0 copy-start.5
  7.2 2.6 stack.2
  9.8 5.8 %all-to-all-start = ((bf16[8,256,576]{1,2,0:T(8,128)(2,1)}), bf16[8,256,576]{1,2,0:T(8,128)(2,1)S(1)}, u32[]{:S(2)}, u32[]{:S(2)}) async-start(bf16[8,256,576]{1,2,0:T(8,128)(2,1)} %stack.2), calls=%async_computation | async-start | bytes 4718592 | tf_op jit(solution)/shard_map/all_to_all | solution.py:13
  15.6 0.0 all-reduce.4.cloned.1.call-start
  15.7 0.0 copy-done.4
  15.7 0.1 add_bitcast_fusion
  15.8 0.0 copy-done.5
  15.8 0.6 dynamic_slice.3
  17.0 1.2 broadcast_compare_fusion
  18.2 27.2 %all-to-all-done = bf16[8,256,576]{1,2,0:T(8,128)(2,1)S(1)} async-done(((bf16[8,256,576]{1,2,0:T(8,128)(2,1)}), bf16[8,256,576]{1,2,0:T(8,128)(2,1)S(1)}, u32[]{:S(2)}, u32[]{:S(2)}) %all-to-all-start) | async-done | bytes 2359328 | tf_op jit(solution)/shard_map/all_to_all | solution.py:13
  45.4 2.7 copy.14
  48.2 5.0 %reshape.65 = bf16[2048,576,1]{0,1,2:T(8,128)(2,1)} reshape(bf16[8,256,576]{1,0,2:T(8,128)(2,1)} %copy.14) | data formatting | bytes 4718592 | tf_op jit(solution)/shard_map/reshape | solution.py:12
  53.2 1.8 copy.29
  54.9 0.0 copy-done
  54.9 10.2 %fusion.10 = (f32[256,4]{0,1:T(4,128)S(1)}, f32[256,4,2048]{2,0,1:T(8,128)}) fusion(pred[256,2048]{1,0:T(8,128)(4,1)} %broadcast_compare_fusion, bf16[256,4,576]{0,2,1:T(8,128)(2,1)S(1)} %copy-done, bf16[2048,576,1]{0,1,2:T(8,128)(2,1)} %reshape.65), kind=kOutput, calls=%fused_computation.24 | convolution fusion | flops 2424309760 | bytes 12455936 | tf_op jit(solution)/shard_map/sub | solution.py:27
  65.1 0.0 copy-start.3
  65.1 4.7 %fusion.5 = bf16[256,4,2048]{2,0,1:T(8,128)(2,1)S(1)} fusion(f32[256,4,2048]{2,0,1:T(8,128)} %get-tuple-element.3, f32[256,4]{0,1:T(4,128)S(1)} %get-tuple-element.2), kind=kLoop, calls=%fused_computation.10 | loop fusion | flops 4194304 | bytes 12587008 | tf_op jit(solution)/shard_map/convert_element_type | solution.py:29
  69.8 0.0 copy-done.3
  69.8 0.0 copy-start.2
  69.9 0.0 slice-start
  69.9 2.4 convolution_bitcast_fusion
  72.3 0.0 copy-done.2
  72.3 0.0 slice-start.1
  72.3 2.5 multiply_reduce_fusion
  74.8 0.0 slice-done
  74.8 0.0 slice-done.1
  74.8 3.4 multiply_convert_fusion
  78.2 0.0 copy-start.6
  78.2 2.1 copy-done.6
  80.3 5.3 %bitcast_add_fusion = f32[2048,576]{1,0:T(8,128)} fusion(f32[2048,512]{1,0:T(8,128)S(1)} %convolution_bitcast_fusion, bf16[256,4,2048]{2,0,1:T(8,128)(2,1)S(1)} %multiply_convert_fusion, bf16[256,4,576]{0,2,1:T(8,128)(2,1)S(1)} %copy-done), kind=kOutput, calls=%fused_computation.5 | convolution fusion | flops 2417098752 | bytes 14286848 | tf_op jit(solution)/shard_map/qhk,qhd->kd/dot_general | solution.py:37
  85.5 0.0 copy-start.1
  85.5 0.0 all-reduce.4.cloned.1.call-update
  85.6 1.6 copy-done.1
  87.2 5.8 %convolution_convert_fusion = bf16[256,4,576]{0,2,1:T(8,128)(2,1)} fusion(bf16[256,4,2048]{2,0,1:T(8,128)(2,1)} %copy-done.6, bf16[2048,576,1]{0,1,2:T(8,128)(2,1)S(1)} %copy-done.1), kind=kOutput, calls=%fused_computation.14 | convolution fusion | flops 2416508928 | bytes 7733248 | tf_op jit(solution)/shard_map/qhk,kd->qhd/dot_general | solution.py:34
  93.0 264.9 %all-reduce.4.cloned.1.call-done = f32[2048,576]{1,0:T(8,128)} async-done(((f32[2048,576]{1,0:T(8,128)}), f32[2048,576]{1,0:T(8,128)}) %all-reduce.4.cloned.1.call-update) | async-done | bytes 4718608
  357.9 1.3 constant_dynamic-slice_fusion
  (4 shorter events, 0.0 us)
Async XLA Ops:
  7.2 47.8 %copy-start = (bf16[256,4,576]{0,2,1:T(8,128)(2,1)S(1)}, bf16[256,4,576]{0,2,1:T(8,128)(2,1)}, u32[]{:S(2)}) copy-start(bf16[256,4,576]{0,2,1:T(8,128)(2,1)} %param.5) | copy-start | bytes 3538948
  7.2 8.5 %copy-start.4 = (s32[8]{0:T(128)S(1)}, s32[8]{0:T(128)}, u32[]{:S(2)}) copy-start(s32[8]{0:T(128)} %param.9) | copy-start | bytes 100
  7.2 8.6 %copy-start.5 = (s32[8]{0:T(128)S(1)}, s32[8]{0:T(128)}, u32[]{:S(2)}) copy-start(s32[8]{0:T(128)} %param.8) | copy-start | bytes 100
  9.8 35.6 %all-to-all-start = ((bf16[8,256,576]{1,2,0:T(8,128)(2,1)}), bf16[8,256,576]{1,2,0:T(8,128)(2,1)S(1)}, u32[]{:S(2)}, u32[]{:S(2)}) async-start(bf16[8,256,576]{1,2,0:T(8,128)(2,1)} %stack.2), calls=%async_computation | async-start | bytes 4718592 | tf_op jit(solution)/shard_map/all_to_all | solution.py:13
  15.6 342.3 %all-reduce.4.cloned.1.call-start = ((), (), s32[]{:S(2)}) async-start(), calls=%async_computation.1 | async-start | bytes 10485760
  65.1 4.7 %copy-start.3 = (bf16[256,4,512]{2,1,0:T(4,128)(2,1)S(1)}, bf16[256,4,512]{2,1,0:T(4,128)(2,1)}, u32[]{:S(2)}) copy-start(bf16[256,4,512]{2,1,0:T(4,128)(2,1)} %param.7) | copy-start | bytes 3145732
  69.8 2.4 copy-start.2
  69.9 5.0 %slice-start = ((s8[8388608]{0:T(1024)(128)(4,1)}), s8[4194304]{0:T(1024)(128)(4,1)S(1)}, s32[]{:S(2)}) async-start(s8[8388608]{0:T(1024)(128)(4,1)} %bitcast.28), calls=%async_computation.2 | async-start | bytes 8388608
  72.3 2.5 slice-start.1
  78.2 2.1 copy-start.6
  85.5 1.7 copy-start.1
Sparse Core Ops, SparseCore 0:
  85.7 272.1 all-reduce.3
